TPU v7x, 512 devices: a whole 4x4x16 slice. The times are simulated.
512 devices in a mesh: ctx: 16 (over z), exp: 32 (over y, x, core).
Axes of the slice: x: 4, y: 4, z: 16, core: 2. Of those that a mesh axis runs over, the one named last changes fastest.
Arguments:
- queries: bfloat16 [1024, 4096], P('ctx', 'exp'), may hold values from -36 to 36
- keys: bfloat16 [1024, 1024], P('ctx'), may hold values from -4 to 4
- values: bfloat16 [1024, 1024], P('ctx'), may hold values from -6 to 6
- out_proj: bfloat16 [4096, 4096], P('ctx', 'exp'), may hold values from -0.09375 to 0.09375
- residual_in: bfloat16 [1024, 4096], P('ctx', 'exp'), may hold values from -48 to 48
- norm_gain: float32 [4096], P('exp'), may hold values from 0.1 to 1.9
- routes: int32 [1024, 2], replicated, may hold values from 0 to 7, all different within a row; in each aligned block of 64 rows (0 to 63, 64 to 127, ...) at most 16 rows name the same one
- gate_wts: float32 [1024, 2], P('ctx'), may hold values from 0.2 to 1
- w_gate: bfloat16 [4096, 65536], P(None, ('exp', 'ctx')), may hold values from -0.09375 to 0.09375
- w_up: bfloat16 [4096, 65536], P(None, ('exp', 'ctx')), may hold values from -0.09375 to 0.09375
- w_down: bfloat16 [65536, 4096], P(('exp', 'ctx')), may hold values from -0.25 to 0.25
Outputs:
- residual_out: bfloat16 [1024, 4096], P('ctx', 'exp')
- expert_out: bfloat16 [1024, 4096], P('ctx', 'exp')
Inputs may be any that keep to these rules, and one draw needn't show every extreme that they name: `routes`: within the 64 tokens of one ctx shard no expert is named more than 16 times, and in every draw some expert is named exactly 16 times within some shard; the two experts of a token differ.
All inputs are finite; a program needn't handle non-finite values.
Results may differ from a plain program's by a relative error of at most 0.033.
Values may be sent and summed in bfloat16 or wider, within the bound.
No kernel may reach another device: no remote copies, remote signals or barrier semaphores. Data moves between devices by JAX's collectives and lax.ppermute only.
A program may use at most 64 MiB of HBM per device.

v0:
```python
import math
import jax
import jax.numpy as jnp
import numpy as np
from jax import lax
from jax.sharding import PartitionSpec as P

D = 4096
QUERY_HEAD_COUNT = 32
KEY_VALUE_HEADS = 8
HEAD_SIZE = 128
EXPERTS = 8
TOP = 2
CAP = 16


def slot_table(routes, shard_count, seg_len):
    flat_routes = routes.reshape(shard_count, seg_len * TOP)
    one_hot = (
        flat_routes[:, :, None] == jnp.arange(EXPERTS, dtype=jnp.int32)[None, None, :]
    ).astype(jnp.int32)
    earlier = jnp.cumsum(one_hot, axis=1) - one_hot
    return (jnp.sum(earlier * one_hot, axis=2), jnp.sum(one_hot, axis=1))


def expert_rows(rows_in, w_gate, w_up, w_down):
    gate_val = jnp.dot(rows_in, w_gate, preferred_element_type=jnp.float32)
    up_val = jnp.dot(rows_in, w_up, preferred_element_type=jnp.float32)
    hidden = (jax.nn.silu(gate_val) * up_val).astype(jnp.bfloat16)
    return jnp.dot(hidden, w_down, preferred_element_type=jnp.float32)


def per_device(
    queries, keys, values, out_proj, residual_in, norm_gain, routes, gate_wts, w_gate, w_up, w_down
):
    ctx_count = lax.axis_size("ctx")
    exp_count = lax.axis_size("exp")
    ctx_rank = lax.axis_index("ctx")
    exp_rank = lax.axis_index("exp")
    seg_len = queries.shape[0]
    heads_dev = queries.shape[1] // HEAD_SIZE
    query_group_width = QUERY_HEAD_COUNT // KEY_VALUE_HEADS
    kv_dev = max(1, heads_dev // query_group_width)
    kv_first = exp_rank * heads_dev // query_group_width
    key_part = lax.dynamic_slice_in_dim(keys, kv_first * HEAD_SIZE, kv_dev * HEAD_SIZE, 1)
    value_part = lax.dynamic_slice_in_dim(values, kv_first * HEAD_SIZE, kv_dev * HEAD_SIZE, 1)
    head_map = np.zeros(heads_dev, dtype=np.int32)
    query_pos = ctx_rank * seg_len + jnp.arange(seg_len, dtype=jnp.int32)
    query_heads = queries.reshape(seg_len, heads_dev, HEAD_SIZE)
    score_scale = 1.0 / math.sqrt(HEAD_SIZE)
    run_max = jnp.full((heads_dev, seg_len), -1e30, jnp.float32)
    run_sum = jnp.zeros((heads_dev, seg_len), jnp.float32)
    run_acc = jnp.zeros((heads_dev, seg_len, HEAD_SIZE), jnp.float32)
    key_piece = lax.all_gather(key_part, "ctx", axis=0, tiled=True)
    value_piece = lax.all_gather(value_part, "ctx", axis=0, tiled=True)
    piece_rows = key_piece.shape[0]
    key_heads = key_piece.reshape(piece_rows, kv_dev, HEAD_SIZE)[:, head_map, :]
    value_heads = value_piece.reshape(piece_rows, kv_dev, HEAD_SIZE)[:, head_map, :]
    scores = (
        jnp.einsum("shd,nhd->hsn", query_heads, key_heads, preferred_element_type=jnp.float32)
        * score_scale
    )
    key_pos = jnp.arange(piece_rows, dtype=jnp.int32)
    visible = (query_pos[:, None] >= key_pos[None, :])[None, :, :]
    scores = jnp.where(visible, scores, -1e30)
    new_max = jnp.maximum(run_max, jnp.max(scores, axis=2))
    weights = jnp.where(visible, jnp.exp(scores - new_max[:, :, None]), 0.0)
    factor = jnp.exp(run_max - new_max)
    new_sum = run_sum * factor + jnp.sum(weights, axis=2)
    added = jnp.einsum(
        "hsn,nhd->hsd",
        weights.astype(jnp.bfloat16),
        value_heads,
        preferred_element_type=jnp.float32,
    )
    run_max, run_sum, run_acc = (new_max, new_sum, run_acc * factor[:, :, None] + added)
    attn_local = (
        (run_acc / run_sum[:, :, None])
        .transpose(1, 0, 2)
        .reshape(seg_len, heads_dev * HEAD_SIZE)
        .astype(jnp.bfloat16)
    )
    attn_all = lax.all_gather(attn_local, "exp", axis=1, tiled=True)
    projected = jnp.dot(
        attn_all,
        lax.all_gather(out_proj, "ctx", axis=0, tiled=True),
        preferred_element_type=jnp.float32,
    )
    residual = residual_in.astype(jnp.float32) + projected
    residual_out = residual.astype(jnp.bfloat16)
    sq_mean = lax.psum(jnp.sum(residual * residual, axis=1), "exp") / D
    normed = (residual * lax.rsqrt(sq_mean + 1e-05)[:, None] * norm_gain[None, :]).astype(
        jnp.bfloat16
    )
    quarters = exp_count // EXPERTS
    my_expert = exp_rank // quarters
    slot_all, counts_all = slot_table(routes, ctx_count, seg_len)
    own_slot = lax.dynamic_index_in_dim(slot_all, ctx_rank, 0, keepdims=False).reshape(seg_len, TOP)
    own_route = lax.dynamic_slice_in_dim(routes, ctx_rank * seg_len, seg_len, 0)
    slot_ids = jnp.arange(CAP, dtype=jnp.int32)
    full_rows = lax.all_gather(normed, "exp", axis=1, tiled=True)
    chosen = (
        ((own_route[None, :, :] == my_expert) & (own_slot[None, :, :] == slot_ids[:, None, None]))
        .astype(jnp.int32)
        .sum(axis=2)
        .astype(jnp.bfloat16)
    )
    picked = jnp.dot(chosen, full_rows, preferred_element_type=jnp.float32).astype(jnp.bfloat16)
    rows_all = lax.all_gather(picked, "ctx", axis=0, tiled=True)
    summed = lax.psum_scatter(
        expert_rows(rows_all, w_gate, w_up, w_down).astype(jnp.bfloat16),
        "ctx",
        scatter_dimension=0,
        tiled=True,
    )
    returned = lax.all_to_all(
        summed.reshape(1, CAP, summed.shape[1]), "exp", split_axis=2, concat_axis=0, tiled=True
    )
    owner_expert = jnp.arange(exp_count, dtype=jnp.int32) // quarters
    match_expert = (own_route[:, :, None] == owner_expert[None, None, :]).astype(jnp.float32)
    match_slot = (own_slot[:, :, None] == slot_ids[None, None, :]).astype(jnp.float32)
    combine = jnp.einsum(
        "tk,tkj,tks->tjs", gate_wts, match_expert, match_slot, precision=lax.Precision.HIGHEST
    ).reshape(seg_len, exp_count * CAP)
    flat_returned = returned.reshape(exp_count * CAP, returned.shape[2]).astype(jnp.float32)
    expert_out = jnp.dot(combine, flat_returned, precision=lax.Precision.HIGHEST).astype(
        jnp.bfloat16
    )
    return (residual_out, expert_out)


def solution(mesh):
    placed = (
        P("ctx", "exp"),
        P("ctx", None),
        P("ctx", None),
        P("ctx", "exp"),
        P("ctx", "exp"),
        P("exp"),
        P(),
        P("ctx", None),
        P(None, ("exp", "ctx")),
        P(None, ("exp", "ctx")),
        P(("exp", "ctx"), None),
    )
    return jax.shard_map(
        per_device,
        mesh=mesh,
        in_specs=placed,
        out_specs=(P("ctx", "exp"), P("ctx", "exp")),
        check_vma=False,
    )
```

profile of v0, /device:TPU:1, one launch (start us, length us, event | category | flops | bytes accessed | tf_op | source)
XLA Modules:
  0.0 401.2 jit_solution(1183322907352983559)
XLA Ops:
  7.2 0.0 copy-start
  7.2 0.0 copy-start.3
  7.2 0.0 all-gather.3.cloned.1.call-start
  7.2 0.7 all-gather.3.cloned.1.call-update
  7.9 0.0 all-gather.5.cloned.1.call-start
  8.0 0.0 copy-start.2
  8.0 0.9 copy.43
  8.9 0.3 eq.66
  9.2 0.1 copy.44
  9.3 2.8 select_reduce_fusion
  12.1 0.2 dynamic-slice_reduce_fusion
  12.3 0.1 eq.70
  12.4 0.1 copy.47
  12.5 0.8 broadcast_compare_fusion
  13.3 0.7 constant_dynamic-slice_fusion.2
  14.0 0.7 constant_dynamic-slice_fusion.1
  14.7 0.0 copy-start.5
  14.7 31.5 %all_gather.18 = bf16[1024,128]{1,0:T(8,128)(2,1)S(1)} all-gather(bf16[64,128]{1,0:T(8,128)(2,1)S(1)} %constant_dynamic-slice_fusion.2), channel_id=1, replica_groups=mesh['ctx'=16,'exp'=32] {'ctx'}, dimensions={0}, use_global_device_ids=true | all-gather | bytes 278528 | tf_op jit(solution)/shard_map/all_gather | solution.py:54
  46.3 21.8 %all_gather.19 = bf16[1024,128]{1,0:T(8,128)(2,1)S(1)} all-gather(bf16[64,128]{1,0:T(8,128)(2,1)S(1)} %constant_dynamic-slice_fusion.1), channel_id=1, replica_groups=mesh['ctx'=16,'exp'=32] {'ctx'}, dimensions={0}, use_global_device_ids=true | all-gather | bytes 278528 | tf_op jit(solution)/shard_map/all_gather | solution.py:55
  68.1 0.0 copy-done.3
  68.1 0.3 fusion.36
  68.4 0.2 fusion.10
  68.6 0.3 fusion.8
  68.9 37.8 %all_gather.20 = bf16[64,4096]{1,0:T(8,128)(2,1)S(1)} all-gather(bf16[64,128]{1,0:T(8,128)(2,1)S(1)} %fusion.8), channel_id=1, replica_groups=mesh['ctx'=16,'exp'=32] {'exp'}, dimensions={1}, use_global_device_ids=true | all-gather | bytes 540672 | tf_op jit(solution)/shard_map/all_gather | solution.py:83
  106.7 0.0 all-gather.3.cloned.1.call-done
  106.7 0.0 copy-done.2
  106.7 1.6 multiply_reduce_fusion
  108.3 62.2 %psum.7 = f32[64]{0:T(128)S(1)} all-reduce(f32[64]{0:T(128)S(1)} %get-tuple-element.10), channel_id=1, replica_groups=mesh['ctx'=16,'exp'=32] {'exp'}, use_global_device_ids=true, to_apply=%region_6.7 | all-reduce | flops 64 | bytes 512 | tf_op jit(solution)/shard_map/psum | solution.py:91
  170.5 0.0 copy-done.5
  170.5 0.6 multiply_convert_fusion
  171.1 25.0 %all_gather.22 = bf16[64,4096]{1,0:T(8,128)(2,1)S(1)} all-gather(bf16[64,128]{1,0:T(8,128)(2,1)S(1)} %get-tuple-element.4), channel_id=1, replica_groups=mesh['ctx'=16,'exp'=32] {'exp'}, dimensions={1}, use_global_device_ids=true | all-gather | bytes 540672 | tf_op jit(solution)/shard_map/all_gather | solution.py:101
  196.1 0.8 convolution_convert_fusion.1
  197.0 0.0 all-gather.5.cloned.1.call-update
  197.0 0.2 reduce-scatter.2.cloned.1.call-start
  197.2 59.8 %all-gather.5.cloned.1.call-done = bf16[256,4096]{1,0:T(8,128)(2,1)} async-done(((bf16[16,4096]{1,0:T(8,128)(2,1)}), bf16[256,4096]{1,0:T(8,128)(2,1)}) %all-gather.5.cloned.1.call-update) | async-done | bytes 2097168 | tf_op jit(solution)/shard_map/all_gather | solution.py:109
  257.0 0.0 copy-start.1
  257.0 2.7 fusion.37
  259.7 0.0 copy-done
  259.7 0.0 copy-done.1
  259.7 3.9 convolution_convert_fusion
  263.6 0.0 copy-start.4
  263.6 0.0 reduce-scatter.2.cloned.1.call-update
  263.7 0.1 copy.42
  263.8 0.6 copy-done.4
  264.3 0.1 copy.45
  264.4 68.4 %reduce-scatter.2.cloned.1.call-done = bf16[16,4096]{1,0:T(8,128)(2,1)} async-done(((bf16[256,4096]{1,0:T(8,128)(2,1)}), bf16[16,4096]{1,0:T(8,128)(2,1)}) %reduce-scatter.2.cloned.1.call-update) | async-done | bytes 131088 | tf_op jit(solution)/shard_map/reduce_scatter | solution.py:110
  332.9 4.3 %copy.48 = bf16[1,16,4096]{1,0,2:T(2,128)(2,1)S(1)} copy(bf16[1,16,4096]{2,1,0:T(8,128)(2,1)} %bitcast.36) | data formatting | bytes 262144 | tf_op jit(solution)/shard_map/reshape | solution.py:117
  337.2 0.5 broadcast.104
  337.7 23.4 %reduce.6 = bf16[4096,16]{1,0:T(8,128)(2,1)} reduce(bf16[4096,1,16]{2,1,0:T(2,128)(2,1)S(1)} %bitcast.30, bf16[]{:T(256)} %broadcast.104), dimensions={1}, to_apply=%bitcast.14.reduce_sub_computation | reduce | bytes 262146
  361.1 3.1 reshape.120
  364.2 17.9 %all-to-all-start = ((bf16[32,2,1024]{2,1,0:T(2,128)(2,1)}), bf16[32,2,1024]{2,1,0:T(2,128)(2,1)S(1)}, u32[]{:S(2)}, u32[]{:S(2)}) async-start(bf16[32,2,1024]{2,1,0:T(2,128)(2,1)} %reshape.120), calls=%async_computation.1 | async-start | bytes 262144 | tf_op jit(solution)/shard_map/all_to_all | solution.py:116
  382.1 0.9 fusion.21
  383.0 0.3 copy.46
  383.3 6.5 %all-to-all-done = bf16[32,2,1024]{2,1,0:T(2,128)(2,1)S(1)} async-done(((bf16[32,2,1024]{2,1,0:T(2,128)(2,1)}), bf16[32,2,1024]{2,1,0:T(2,128)(2,1)S(1)}, u32[]{:S(2)}, u32[]{:S(2)}) %all-to-all-start) | async-done | bytes 131104 | tf_op jit(solution)/shard_map/all_to_all | solution.py:116
  389.7 1.8 reshape.121
  391.6 2.0 copy.49
  393.6 0.1 copy.50
  393.7 1.0 convolution_convert_fusion.2
  (8 shorter events, 0.1 us)
Async XLA Ops:
  7.2 252.6 %copy-start = (bf16[128,4096]{1,0:T(8,128)(2,1)S(1)}, bf16[128,4096]{1,0:T(8,128)(2,1)}, u32[]{:S(2)}) copy-start(bf16[128,4096]{1,0:T(8,128)(2,1)} %param.24) | copy-start | bytes 3145732
  7.2 60.9 %copy-start.3 = (bf16[64,128]{1,0:T(8,128)(2,1)S(1)}, bf16[64,128]{1,0:T(8,128)(2,1)}, u32[]{:S(2)}) copy-start(bf16[64,128]{1,0:T(8,128)(2,1)} %param.14) | copy-start | bytes 49156
  7.2 99.5 %all-gather.3.cloned.1.call-start = ((), (), s32[]{:S(2)}) async-start(), calls=%async_computation.2 | async-start | bytes 1114112 | tf_op jit(solution)/shard_map/all_gather | solution.py:86
  7.9 249.1 %all-gather.5.cloned.1.call-start = ((), (), s32[]{:S(2)}) async-start(), calls=%async_computation.3 | async-start | bytes 2228224 | tf_op jit(solution)/shard_map/all_gather | solution.py:109
  8.0 98.7 %copy-start.2 = (bf16[64,128]{1,0:T(8,128)(2,1)S(1)}, bf16[64,128]{1,0:T(8,128)(2,1)}, u32[]{:S(2)}) copy-start(bf16[64,128]{1,0:T(8,128)(2,1)} %param.18) | copy-start | bytes 49156
  14.7 155.8 %copy-start.5 = (f32[128]{0:T(128)S(1)}, f32[128]{0:T(128)}, u32[]{:S(2)}) copy-start(f32[128]{0:T(128)} %param.19) | copy-start | bytes 1540
  197.0 135.8 %reduce-scatter.2.cloned.1.call-start = ((), (), s32[]{:S(2)}) async-start(), calls=%async_computation.4 | async-start | bytes 2228224 | tf_op jit(solution)/shard_map/reduce_scatter | solution.py:110
  257.0 2.7 copy-start.1
  263.6 0.7 copy-start.4
  364.2 25.5 %all-to-all-start = ((bf16[32,2,1024]{2,1,0:T(2,128)(2,1)}), bf16[32,2,1024]{2,1,0:T(2,128)(2,1)S(1)}, u32[]{:S(2)}, u32[]{:S(2)}) async-start(bf16[32,2,1024]{2,1,0:T(2,128)(2,1)} %reshape.120), calls=%async_computation.1 | async-start | bytes 262144 | tf_op jit(solution)/shard_map/all_to_all | solution.py:116
Sparse Core Ops, SparseCore 0:
  10.1 66.9 all-gather.2
  197.1 59.8 all-gather.4
  263.8 69.0 reduce-scatter.1
where the time goes:
time: 402 us; the launch traced here: 401 us
  blocking collectives  178 us (44%)
  waiting for transfers between devices  135 us (34%)
  other arithmetic  27.9 us (7%)
  starting transfers between devices  18.2 us (5%)
  local copies, waits for them, and re-layouts  16 us (4%)
  between operations  13.9 us (3%)
  matrix products  11.5 us (3%)
    reduce_scatter x1, waiting for transfers between devices, per_device(): lax.psum_scatter(expert_rows(rows_all, w_gate, w_up, w_down).astype(jnp.b...  68.4 us
    psum x1, blocking collectives, per_device(): sq_mean = lax.psum(jnp.sum(residual * residual, axis=1), 'exp') / D  62.2 us
    all_gather x1, waiting for transfers between devices, per_device(): rows_all = lax.all_gather(picked, 'ctx', axis=0, tiled=True)  59.8 us
    all_gather x1, blocking collectives, per_device(): attn_all = lax.all_gather(attn_local, 'exp', axis=1, tiled=True)  37.8 us
    all_gather x1, blocking collectives, per_device(): key_piece = lax.all_gather(key_part, 'ctx', axis=0, tiled=True)  31.5 us
    all_gather x1, blocking collectives, per_device(): full_rows = lax.all_gather(normed, 'exp', axis=1, tiled=True)  25 us
    unnamed x1, other arithmetic  23.4 us
    all_gather x1, blocking collectives, per_device(): value_piece = lax.all_gather(value_part, 'ctx', axis=0, tiled=True)  21.8 us
  transfers between devices with their start and end apart: 4, of which 3 were waited for; matrix products, arithmetic and copies ran while one was open for 2% of the time, Pallas kernels for 0%

commit v1 on v0

--- a/solution.py
+++ b/solution.py
@@ -4,6 +4,7 @@
 import numpy as np
 from jax import lax
 from jax.sharding import PartitionSpec as P
+from jax.lax import all_gather
 
 D = 4096
 QUERY_HEAD_COUNT = 32
@@ -12,6 +13,11 @@
 EXPERTS = 8
 TOP = 2
 CAP = 16
+store_heaps = lambda v0, patch: jnp.split(
+    all_gather(jnp.concatenate([v0, patch], 1), axis_name="ctx", axis=0, tiled=True),
+    [v0.shape[1]],
+    1,
+)
 
 
 def slot_table(routes, shard_count, seg_len):
@@ -51,8 +57,7 @@
     run_max = jnp.full((heads_dev, seg_len), -1e30, jnp.float32)
     run_sum = jnp.zeros((heads_dev, seg_len), jnp.float32)
     run_acc = jnp.zeros((heads_dev, seg_len, HEAD_SIZE), jnp.float32)
-    key_piece = lax.all_gather(key_part, "ctx", axis=0, tiled=True)
-    value_piece = lax.all_gather(value_part, "ctx", axis=0, tiled=True)
+    key_piece, value_piece = store_heaps(key_part, value_part)
     piece_rows = key_piece.shape[0]
     key_heads = key_piece.reshape(piece_rows, kv_dev, HEAD_SIZE)[:, head_map, :]
     value_heads = value_piece.reshape(piece_rows, kv_dev, HEAD_SIZE)[:, head_map, :]

time: 402 us -> 379 us (0.943)
  blocking collectives: 178 us -> 157 us
    all_gather x2 -> x1, blocking collectives: 53.3 us -> 33.2 us  [all_gather(jnp.concatenate([v0, patch], 1), axis_name='ctx', axis=0, tile...]
    psum x1, blocking collectives: 62.2 us -> 68.2 us  [per_device(): sq_mean = lax.psum(jnp.sum(residual * residual, axis=1), 'exp') / D]
    all_gather x1, blocking collectives: 37.8 us -> 33.1 us  [per_device(): attn_all = lax.all_gather(attn_local, 'exp', axis=1, tiled=True)]
where the time goes in v1:
time: 379 us; the launch traced here: 378 us
  blocking collectives  157 us (41%)
  waiting for transfers between devices  134 us (35%)
  other arithmetic  27.9 us (7%)
  starting transfers between devices  18.3 us (5%)
  local copies, waits for them, and re-layouts  15.3 us (4%)
  between operations  13.9 us (4%)
  matrix products  11.5 us (3%)
    reduce_scatter x1, waiting for transfers between devices, per_device(): lax.psum_scatter(expert_rows(rows_all, w_gate, w_up, w_down).astype(jnp.b...  68.3 us
    psum x1, blocking collectives, per_device(): sq_mean = lax.psum(jnp.sum(residual * residual, axis=1), 'exp') / D  68.2 us
    all_gather x1, waiting for transfers between devices, per_device(): rows_all = lax.all_gather(picked, 'ctx', axis=0, tiled=True)  58.9 us
    all_gather x1, blocking collectives, all_gather(jnp.concatenate([v0, patch], 1), axis_name='ctx', axis=0, tile...  33.2 us
    all_gather x1, blocking collectives, per_device(): attn_all = lax.all_gather(attn_local, 'exp', axis=1, tiled=True)  33.1 us
    unnamed x1, other arithmetic  23.4 us
    all_gather x1, blocking collectives, per_device(): full_rows = lax.all_gather(normed, 'exp', axis=1, tiled=True)  22.4 us
    all_to_all x1, starting transfers between devices, per_device(): lax.all_to_all(summed.reshape(1, CAP, summed.shape[1]), 'exp', split_axis...  18 us
  transfers between devices with their start and end apart: 4, of which 3 were waited for; matrix products, arithmetic and copies ran while one was open for 2% of the time, Pallas kernels for 0%

profile of v1, /device:TPU:1, one launch (start us, length us, event | category | flops | bytes accessed | tf_op | source)
XLA Modules:
  0.0 378.1 jit_solution(2140738698841987422)
XLA Ops:
  7.2 0.0 copy-start
  7.2 0.0 copy-start.5
  7.2 0.0 all-gather.3.cloned.1.call-start
  7.2 0.7 all-gather.3.cloned.1.call-update
  7.9 0.0 all-gather.5.cloned.1.call-start
  8.0 0.9 copy.43
  8.9 0.0 copy-start.2
  8.9 0.3 eq.66
  9.2 0.1 copy.44
  9.3 2.8 select_reduce_fusion
  12.1 0.2 dynamic-slice_reduce_fusion
  12.3 0.1 eq.70
  12.4 0.1 copy.47
  12.5 0.8 broadcast_compare_fusion
  13.3 0.7 constant_dynamic-slice_fusion.1
  14.0 33.2 %all_gather.15 = bf16[1024,256]{1,0:T(8,128)(2,1)S(1)} all-gather(bf16[64,256]{1,0:T(8,128)(2,1)S(1)} %pad_maximum_fusion), channel_id=1, replica_groups=mesh['ctx'=16,'exp'=32] {'ctx'}, dimensions={0}, use_global_device_ids=true | all-gather | bytes 557056 | tf_op jit(solution)/shard_map/all_gather | solution.py:17
  47.2 0.0 copy-done.5
  47.2 0.0 copy-start.4
  47.2 0.3 fusion.38
  47.5 0.2 fusion.12
  47.8 0.3 fusion.8
  48.0 33.1 %all_gather.16 = bf16[64,4096]{1,0:T(8,128)(2,1)S(1)} all-gather(bf16[64,128]{1,0:T(8,128)(2,1)S(1)} %fusion.8), channel_id=1, replica_groups=mesh['ctx'=16,'exp'=32] {'exp'}, dimensions={1}, use_global_device_ids=true | all-gather | bytes 540672 | tf_op jit(solution)/shard_map/all_gather | solution.py:88
  81.1 0.0 all-gather.3.cloned.1.call-done
  81.1 0.0 copy-done.2
  81.1 1.6 multiply_reduce_fusion
  82.8 68.2 %psum.7 = f32[64]{0:T(128)S(1)} all-reduce(f32[64]{0:T(128)S(1)} %get-tuple-element.10), channel_id=1, replica_groups=mesh['ctx'=16,'exp'=32] {'exp'}, use_global_device_ids=true, to_apply=%region_6.7 | all-reduce | flops 64 | bytes 512 | tf_op jit(solution)/shard_map/psum | solution.py:96
  151.0 0.0 copy-done.4
  151.0 0.6 multiply_convert_fusion
  151.6 22.4 %all_gather.18 = bf16[64,4096]{1,0:T(8,128)(2,1)S(1)} all-gather(bf16[64,128]{1,0:T(8,128)(2,1)S(1)} %get-tuple-element.4), channel_id=1, replica_groups=mesh['ctx'=16,'exp'=32] {'exp'}, dimensions={1}, use_global_device_ids=true | all-gather | bytes 540672 | tf_op jit(solution)/shard_map/all_gather | solution.py:106
  174.0 0.8 convolution_convert_fusion.1
  174.8 0.0 all-gather.5.cloned.1.call-update
  174.8 0.2 reduce-scatter.2.cloned.1.call-start
  175.1 58.9 %all-gather.5.cloned.1.call-done = bf16[256,4096]{1,0:T(8,128)(2,1)} async-done(((bf16[16,4096]{1,0:T(8,128)(2,1)}), bf16[256,4096]{1,0:T(8,128)(2,1)}) %all-gather.5.cloned.1.call-update) | async-done | bytes 2097168 | tf_op jit(solution)/shard_map/all_gather | solution.py:114
  234.0 0.0 copy-start.1
  234.0 2.7 fusion.39
  236.7 0.0 copy-done
  236.7 0.0 copy-done.1
  236.7 3.9 %convolution_convert_fusion = bf16[256,4096]{1,0:T(8,128)(2,1)} fusion(bf16[128,4096]{1,0:T(8,128)(2,1)S(1)} %copy-done, bf16[256,4096]{1,0:T(8,128)(2,1)S(1)} %copy-done.1, bf16[4096,128]{1,0:T(8,128)(2,1)} %param.23, f32[256,128]{1,0:T(8,128)S(1)} %fusion.39), kind=kOutput, calls=%fused_computation | convolution fusion | flops 538116096 | bytes 6422528 | tf_op jit(solution)/shard_map/dot_general | solution.py:36
  240.6 0.0 copy-start.3
  240.6 0.0 reduce-scatter.2.cloned.1.call-update
  240.6 0.1 copy.42
  240.7 0.6 copy-done.3
  241.3 0.1 copy.45
  241.4 68.3 %reduce-scatter.2.cloned.1.call-done = bf16[16,4096]{1,0:T(8,128)(2,1)} async-done(((bf16[256,4096]{1,0:T(8,128)(2,1)}), bf16[16,4096]{1,0:T(8,128)(2,1)}) %reduce-scatter.2.cloned.1.call-update) | async-done | bytes 131088 | tf_op jit(solution)/shard_map/reduce_scatter | solution.py:115
  309.7 4.3 %copy.48 = bf16[1,16,4096]{1,0,2:T(2,128)(2,1)S(1)} copy(bf16[1,16,4096]{2,1,0:T(8,128)(2,1)} %bitcast.34) | data formatting | bytes 262144 | tf_op jit(solution)/shard_map/reshape | solution.py:122
  314.0 0.5 broadcast.104
  314.5 23.4 %reduce.6 = bf16[4096,16]{1,0:T(8,128)(2,1)} reduce(bf16[4096,1,16]{2,1,0:T(2,128)(2,1)S(1)} %bitcast.28, bf16[]{:T(256)} %broadcast.104), dimensions={1}, to_apply=%bitcast.14.reduce_sub_computation | reduce | bytes 262146
  337.9 3.1 reshape.120
  341.0 18.0 %all-to-all-start = ((bf16[32,2,1024]{2,1,0:T(2,128)(2,1)}), bf16[32,2,1024]{2,1,0:T(2,128)(2,1)S(1)}, u32[]{:S(2)}, u32[]{:S(2)}) async-start(bf16[32,2,1024]{2,1,0:T(2,128)(2,1)} %reshape.120), calls=%async_computation.1 | async-start | bytes 262144 | tf_op jit(solution)/shard_map/all_to_all | solution.py:121
  359.1 0.9 fusion.23
  359.9 0.3 copy.46
  360.2 6.5 %all-to-all-done = bf16[32,2,1024]{2,1,0:T(2,128)(2,1)S(1)} async-done(((bf16[32,2,1024]{2,1,0:T(2,128)(2,1)}), bf16[32,2,1024]{2,1,0:T(2,128)(2,1)S(1)}, u32[]{:S(2)}, u32[]{:S(2)}) %all-to-all-start) | async-done | bytes 131104 | tf_op jit(solution)/shard_map/all_to_all | solution.py:121
  366.7 1.8 reshape.121
  368.5 2.0 copy.49
  370.6 0.1 copy.50
  370.6 1.0 convolution_convert_fusion.2
  (9 shorter events, 0.1 us)
Async XLA Ops:
  7.2 229.5 %copy-start = (bf16[128,4096]{1,0:T(8,128)(2,1)S(1)}, bf16[128,4096]{1,0:T(8,128)(2,1)}, u32[]{:S(2)}) copy-start(bf16[128,4096]{1,0:T(8,128)(2,1)} %param.24) | copy-start | bytes 3145732
  7.2 40.0 %copy-start.5 = (bf16[64,128]{1,0:T(8,128)(2,1)S(1)}, bf16[64,128]{1,0:T(8,128)(2,1)}, u32[]{:S(2)}) copy-start(bf16[64,128]{1,0:T(8,128)(2,1)} %param.14) | copy-start | bytes 49156
  7.2 74.0 %all-gather.3.cloned.1.call-start = ((), (), s32[]{:S(2)}) async-start(), calls=%async_computation.2 | async-start | bytes 1114112 | tf_op jit(solution)/shard_map/all_gather | solution.py:91
  7.9 226.1 %all-gather.5.cloned.1.call-start = ((), (), s32[]{:S(2)}) async-start(), calls=%async_computation.3 | async-start | bytes 2228224 | tf_op jit(solution)/shard_map/all_gather | solution.py:114
  8.9 72.2 %copy-start.2 = (bf16[64,128]{1,0:T(8,128)(2,1)S(1)}, bf16[64,128]{1,0:T(8,128)(2,1)}, u32[]{:S(2)}) copy-start(bf16[64,128]{1,0:T(8,128)(2,1)} %param.18) | copy-start | bytes 49156
  47.2 103.8 %copy-start.4 = (f32[128]{0:T(128)S(1)}, f32[128]{0:T(128)}, u32[]{:S(2)}) copy-start(f32[128]{0:T(128)} %param.19) | copy-start | bytes 1540
  174.8 134.8 %reduce-scatter.2.cloned.1.call-start = ((), (), s32[]{:S(2)}) async-start(), calls=%async_computation.4 | async-start | bytes 2228224 | tf_op jit(solution)/shard_map/reduce_scatter | solution.py:115
  234.0 2.7 copy-start.1
  240.6 0.7 copy-start.3
  341.0 25.7 %all-to-all-start = ((bf16[32,2,1024]{2,1,0:T(2,128)(2,1)}), bf16[32,2,1024]{2,1,0:T(2,128)(2,1)S(1)}, u32[]{:S(2)}, u32[]{:S(2)}) async-start(bf16[32,2,1024]{2,1,0:T(2,128)(2,1)} %reshape.120), calls=%async_computation.1 | async-start | bytes 262144 | tf_op jit(solution)/shard_map/all_to_all | solution.py:121
Sparse Core Ops, SparseCore 0:
  10.1 66.7 all-gather.2
  175.0 58.9 all-gather.4
  240.8 68.8 reduce-scatter.1
